TPU v7x, 32 devices: a whole 2x2x4 slice. The times are simulated.
32 devices in a mesh: wide: 16 (over z, y, x), narrow: 2 (over core).
Axes of the slice: x: 2, y: 2, z: 4, core: 2. Of those that a mesh axis runs over, the one named last changes fastest.
Arguments:
- frames: bfloat16 [4096, 1024], P('wide'), may hold values from -6 to 6
- expert_ids: int32 [4096, 2], P('wide'), may hold values from 0 to 15, all different within a row; in each aligned block of 256 rows (0 to 255, 256 to 511, ...) at most 64 rows name the same one
- gate_values: float32 [4096, 2], P('wide'), may hold values from 0.1 to 1
- w_gate: bfloat16 [16, 1024, 4096], P('wide', None, 'narrow'), may hold values from -0.1875 to 0.1875
- w_up: bfloat16 [16, 1024, 4096], P('wide', None, 'narrow'), may hold values from -0.1875 to 0.1875
- w_down: bfloat16 [16, 4096, 1024], P('wide', 'narrow'), may hold values from -0.09375 to 0.09375
- norm_gain: float32 [1024], replicated, may hold values from 0.1 to 1.9
- norm_bias: float32 [1024], replicated, may hold values from -2 to 2
- point_in: bfloat16 [1024, 2, 1024], P(None, None, 'narrow'), may hold values from -0.1875 to 0.1875
- depth_kernel: bfloat16 [31, 1024], P(None, 'narrow'), may hold values from -1 to 1
- point_out: bfloat16 [1024, 1024], P('narrow'), may hold values from -0.1875 to 0.1875
Outputs:
- block_out: bfloat16 [4096, 1024], P(('wide', 'narrow'))
Inputs may be any that keep to these rules, and one draw needn't show every extreme that they name: `expert_ids`: each frame names 2 different experts; in each aligned block of 256 frames no expert is named by more than 64 frames, and every expert is named somewhere.
All inputs are finite; a program needn't handle non-finite values.
Results may differ from a plain program's by a relative error of at most 0.015.
Values may be sent and summed in bfloat16 or wider, within the bound.
A program may use at most 64 MiB of HBM per device.

v0:
```python
import jax
import jax.numpy as jnp
from jax import lax
from jax.sharding import PartitionSpec as P


def padded_2(cells, sides, width):
    for axis, dim in sides:
        count = lax.axis_size(axis)
        ends = count - 1
        head = lax.slice_in_dim(cells, 0, width, axis=dim)
        tail = lax.slice_in_dim(cells, cells.shape[dim] - width, cells.shape[dim], axis=dim)
        cells = jnp.concatenate(
            [
                lax.ppermute(tail, axis, [(i, (i + 1) % count) for i in range(ends)]),
                cells,
                lax.ppermute(head, axis, [((i + 1) % count, i) for i in range(ends)]),
            ],
            axis=dim,
        )
    return cells


def shards(
    frames,
    expert_ids,
    gate_values,
    w_gate,
    w_up,
    w_down,
    norm_gain,
    norm_bias,
    point_in,
    depth_kernel,
    point_out,
):
    frame_count = frames.shape[0]
    model_width = frames.shape[1]
    top_count = expert_ids.shape[1]
    wide_count = lax.axis_size("wide")
    narrow_count = lax.axis_size("narrow")
    local_experts = w_gate.shape[0]
    expert_count = local_experts * wide_count
    capacity = 2 * top_count * frame_count // expert_count
    flat_ids = expert_ids.reshape(-1)
    one_hot = (flat_ids[:, None] == jnp.arange(expert_count, dtype=jnp.int32)[None, :]).astype(
        jnp.int32
    )
    running = jnp.cumsum(one_hot, axis=0)
    slot_index = jnp.sum((running - 1) * one_hot, axis=1)
    target_row = flat_ids * capacity + slot_index
    repeated = jnp.repeat(frames, top_count, axis=0)
    outgoing = (
        jnp.zeros((expert_count * capacity, model_width), jnp.bfloat16).at[target_row].set(repeated)
    )
    outgoing = outgoing.reshape(expert_count, capacity, model_width)
    arrived = lax.all_to_all(outgoing, "wide", split_axis=0, concat_axis=0, tiled=True)
    arrived = arrived.reshape(wide_count, local_experts, capacity, model_width)
    gate_h = jnp.einsum("sjcd,jdf->sjcf", arrived, w_gate, preferred_element_type=jnp.float32)
    up_h = jnp.einsum("sjcd,jdf->sjcf", arrived, w_up, preferred_element_type=jnp.float32)
    hidden = (jax.nn.silu(gate_h) * up_h).astype(jnp.bfloat16)
    partial_value = jnp.einsum(
        "sjcf,jfd->sjcd", hidden, w_down, preferred_element_type=jnp.float32
    ).astype(jnp.bfloat16)
    partial_value = partial_value.reshape(wide_count * local_experts, capacity, model_width)
    returned = lax.all_to_all(partial_value, "wide", split_axis=0, concat_axis=0, tiled=True)
    picked = jnp.take(returned.reshape(expert_count * capacity, model_width), target_row, axis=0)
    picked = picked.reshape(frame_count, top_count, model_width)
    mixture = jnp.sum(gate_values[:, :, None] * picked.astype(jnp.float32), axis=1)
    moe_sum = lax.psum(mixture.astype(jnp.bfloat16), "narrow").astype(jnp.float32)
    residual = frames.astype(jnp.float32) + moe_sum
    row_mean = jnp.mean(residual, axis=1, keepdims=True)
    centered = residual - row_mean
    row_var = jnp.mean(centered * centered, axis=1, keepdims=True)
    normed = (
        centered / jnp.sqrt(row_var + 1e-05) * norm_gain[None, :] + norm_bias[None, :]
    ).astype(jnp.bfloat16)
    channels = point_in.shape[2]
    projected = jnp.dot(
        normed, point_in.reshape(model_width, 2 * channels), preferred_element_type=jnp.float32
    )
    value_half = projected[:, :channels]
    gate_half = projected[:, channels:]
    glu_out = (value_half * jax.nn.sigmoid(gate_half)).astype(jnp.bfloat16)
    taps_count = depth_kernel.shape[0]
    half_width = (taps_count - 1) // 2
    padded = padded_2(glu_out, (("wide", 0),), half_width)
    depthwise = jnp.zeros((frame_count, channels), jnp.float32)
    for tap_index in range(taps_count):
        depthwise = (
            depthwise
            + padded[tap_index : tap_index + frame_count].astype(jnp.float32)
            * depth_kernel[tap_index].astype(jnp.float32)[None, :]
        )
    activated = (depthwise * jax.nn.sigmoid(depthwise)).astype(jnp.bfloat16)
    share_rows = frame_count // narrow_count
    summed = lax.psum_scatter(
        jnp.dot(activated, point_out, preferred_element_type=jnp.float32).astype(jnp.bfloat16),
        "narrow",
        scatter_dimension=0,
        tiled=True,
    ).astype(jnp.float32)
    own_rows = lax.dynamic_slice_in_dim(
        residual, lax.axis_index("narrow") * share_rows, share_rows, 0
    )
    return (own_rows + summed).astype(jnp.bfloat16)


def solution(mesh):
    return jax.shard_map(
        shards,
        mesh=mesh,
        in_specs=(
            P("wide", None),
            P("wide", None),
            P("wide", None),
            P("wide", None, "narrow"),
            P("wide", None, "narrow"),
            P("wide", "narrow", None),
            P(),
            P(),
            P(None, None, "narrow"),
            P(None, "narrow"),
            P("narrow", None),
        ),
        out_specs=P(("wide", "narrow"), None),
        check_vma=False,
    )
```

profile of v0, /device:TPU:0, one launch (start us, length us, event | category | flops | bytes accessed | tf_op | source)
XLA Modules:
  0.0 215.9 jit_solution(2543223562741324651)
XLA Ops:
  6.5 0.0 copy-start
  6.5 0.9 copy.20
  7.4 0.1 eq.26
  7.6 0.1 reshape.113
  7.7 0.7 broadcast_multiply_fusion
  8.4 1.1 reduce-window.6
  9.6 0.2 slice_reduce_fusion
  9.8 0.1 copy.25
  10.0 0.1 mul.464
  10.1 1.6 broadcast_in_dim.16
  11.7 1.2 reshape.166
  13.0 0.1 fusion.62
  13.1 3.9 %scatter_custom_fusion = bf16[1024,1024]{1,0:T(8,128)(2,1)S(1)} fusion(s32[512]{0:T(512)S(1)} %bitcast.123, bf16[512,1024]{1,0:T(8,128)(2,1)} %reshape.166, bf16[]{:T(256)} %constant.21.clone.1), kind=kCustom, calls=%fused_computation.50 | custom fusion | bytes 2097664 | tf_op jit(solution)/shard_map/scatter | solution.py:54
  17.0 0.0 copy-start.6
  17.0 57.2 %all_to_all.10 = bf16[16,64,1024]{2,1,0:T(8,128)(2,1)S(1)} all-to-all(bf16[16,64,1024]{2,1,0:T(8,128)(2,1)S(1)} %bitcast.119), channel_id=1, replica_groups=mesh['wide'=16,'narrow'=2] {'wide'}, dimensions={0} | all-to-all | bytes 4194304 | tf_op jit(solution)/shard_map/all_to_all | solution.py:57
  74.2 1.4 copy-done.2
  75.6 0.0 copy-done.6
  75.6 6.6 %fusion.8 = f32[16,64,2048]{2,1,0:T(8,128)} fusion(bf16[16,64,1024]{2,1,0:T(8,128)(2,1)S(1)} %all_to_all.10, bf16[1,1024,2048]{2,1,0:T(8,128)(2,1)S(1)} %copy-done.6), kind=kOutput, calls=%fused_computation.13 | convolution fusion | flops 4294967296 | bytes 14680064 | tf_op jit(solution)/shard_map/sjcd,jdf->sjcf/dot_general | solution.py:59
  82.2 16.6 %fusion.14 = bf16[16,64,1024]{2,1,0:T(8,128)(2,1)} fusion(bf16[1,2048,1024]{2,1,0:T(8,128)(2,1)} %param.16, bf16[16,64,1024]{2,1,0:T(8,128)(2,1)} %copy-done.2, bf16[1,1024,2048]{2,1,0:T(8,128)(2,1)} %param.15, f32[16,64,2048]{2,1,0:T(8,128)} %fusion.8), kind=kOutput, calls=%fused_computation.17 | convolution fusion | flops 8603566080 | bytes 20971520 | tf_op jit(solution)/shard_map/sjcf,jfd->sjcd/dot_general | solution.py:62
  98.8 4.0 %all-to-all-start.1 = ((bf16[16,64,1024]{2,1,0:T(8,128)(2,1)}), bf16[16,64,1024]{2,1,0:T(8,128)(2,1)S(1)}, u32[]{:S(2)}, u32[]{:S(2)}) async-start(bf16[16,64,1024]{2,1,0:T(8,128)(2,1)} %fusion.14), calls=%async_computation.1 | async-start | bytes 4194304 | tf_op jit(solution)/shard_map/all_to_all | solution.py:66
  102.9 0.0 all-reduce.2.cloned.1.call-start
  102.9 0.1 reduce_sum.41
  103.1 0.1 copy.23
  103.1 0.0 copy-done.4
  103.2 0.2 copy.24
  103.3 0.0 copy-done.5
  103.4 0.1 copy.19
  103.5 41.9 %all-to-all-done.1 = bf16[16,64,1024]{2,1,0:T(8,128)(2,1)S(1)} async-done(((bf16[16,64,1024]{2,1,0:T(8,128)(2,1)}), bf16[16,64,1024]{2,1,0:T(8,128)(2,1)S(1)}, u32[]{:S(2)}, u32[]{:S(2)}) %all-to-all-start.1) | async-done | bytes 2097184 | tf_op jit(solution)/shard_map/all_to_all | solution.py:66
  145.4 2.8 %gather_fusion = bf16[512,1024]{1,0:T(8,128)(2,1)} fusion(bf16[1024,1024]{1,0:T(8,128)(2,1)S(1)} %bitcast.118, s32[1024]{0:T(1024)S(1)} %pad_clamp_fusion), kind=kCustom, calls=%fused_computation | custom fusion | bytes 2099200 | tf_op jit(solution)/shard_map/jit(_take)/gather | solution.py:67
  148.2 1.5 gather.7
  149.8 5.0 %multiply_reduce_fusion = bf16[256,1024]{1,0:T(8,128)(2,1)} fusion(bf16[256,2,1024]{2,1,0:T(2,128)(2,1)S(1)} %gather.7, pred[256,2]{1,0:T(8,128)(4,1)S(1)} %copy.24, f32[256,2]{1,0:T(8,128)S(1)} %copy.19), kind=kLoop, calls=%fused_computation.15 | loop fusion | flops 1835008 | bytes 1575424 | tf_op jit(solution)/shard_map/reduce_sum | solution.py:69
  154.8 0.0 all-reduce.2.cloned.1.call-update
  154.8 0.3 reduce-scatter.2.cloned.1.call-start
  155.1 3.5 %copy.27 = bf16[128,8,2,512]{3,1,2,0:T(8,128)(2,1)} copy(bf16[128,8,2,512]{3,2,1,0:T(2,128)(2,1)} %bitcast.120) | data formatting | bytes 4194304
  158.6 19.2 %all-reduce.2.cloned.1.call-done = bf16[256,1024]{1,0:T(8,128)(2,1)} async-done(((bf16[256,1024]{1,0:T(8,128)(2,1)}), bf16[256,1024]{1,0:T(8,128)(2,1)}) %all-reduce.2.cloned.1.call-update) | async-done | bytes 524304 | tf_op jit(solution)/shard_map/psum | solution.py:70
  177.8 1.3 convert_add_fusion
  179.1 1.3 multiply_reduce_fusion.1
  180.5 0.0 copy-done.8
  180.5 2.5 %fusion.23 = f32[256,1024]{1,0:T(8,128)S(1)} fusion(bf16[1024,1024]{1,0:T(8,128)(2,1)} %bitcast.121, f32[1024]{0:T(1024)S(1)} %copy-done.7, f32[1024]{0:T(1024)S(1)} %copy-done.8, f32[256]{0:T(256)S(1)} %add_sqrt_fusion, f32[256]{0:T(256)S(1)} %broadcast_multiply_fusion.1, bf16[256,1024]{1,0:T(8,128)(2,1)} %all-reduce.2.cloned.1.call-done, ...), kind=kOutput, calls=%fused_computation.52 | convolution fusion | flops 538968064 | bytes 4204544 | tf_op jit(solution)/shard_map/dot_general | solution.py:79
  183.0 0.1 fusion.32
  183.2 3.6 %collective-permute-start = (bf16[15,512]{1,0:T(8,128)(2,1)S(1)}, bf16[15,512]{1,0:T(8,128)(2,1)S(1)}, u32[]{:S(2)}, u32[]{:S(2)}) collective-permute-start(bf16[15,512]{1,0:T(8,128)(2,1)S(1)} %get-tuple-element.7), channel_id=1, source_target_pairs={{0,2},{2,4},{4,6},{6,8},{8,10},{10,12},{12,14},{14,16},{16,18},{18... | collective-permute-start | bytes 46088 | tf_op jit(solution)/shard_map/ppermute | solution.py:15
  186.9 1.3 collective-permute-start.1
  188.2 0.1 collective-permute-done
  188.3 4.2 %collective-permute-done.1 = bf16[15,512]{1,0:T(8,128)(2,1)S(1)} collective-permute-done((bf16[15,512]{1,0:T(8,128)(2,1)S(1)}, bf16[15,512]{1,0:T(8,128)(2,1)S(1)}, u32[]{:S(2)}, u32[]{:S(2)}) %collective-permute-start.1) | collective-permute-done | bytes 15392 | tf_op jit(solution)/shard_map/ppermute | solution.py:17
  192.5 5.0 %convolution_convert_fusion = bf16[256,1024]{1,0:T(8,128)(2,1)} fusion(bf16[512,1024]{1,0:T(8,128)(2,1)S(1)} %copy-done, bf16[256,512]{1,0:T(8,128)(2,1)S(1)} %fusion.32, bf16[15,512]{1,0:T(8,128)(2,1)S(1)} %collective-permute-done.1, bf16[15,512]{1,0:T(8,128)(2,1)S(1)} %collective-permute-done, f32[512]{0:T(512)S(1)} %bitcast.154, f32[512]{0:T(512)S(1)} %bitcast.155, ...), kind=kOutput, calls=%fused_computation.46 | convolution fusion | flops 293208064 | bytes 1929216 | tf_op jit(solution)/shard_map/dot_general | solution.py:98
  197.4 0.0 reduce-scatter.2.cloned.1.call-update
  197.5 9.9 %reduce-scatter.2.cloned.1.call-done = bf16[128,1024]{1,0:T(8,128)(2,1)} async-done(((bf16[256,1024]{1,0:T(8,128)(2,1)}), bf16[128,1024]{1,0:T(8,128)(2,1)}) %reduce-scatter.2.cloned.1.call-update) | async-done | bytes 262160 | tf_op jit(solution)/shard_map/reduce_scatter | solution.py:97
  207.4 1.7 add_convert_fusion.2
  (22 shorter events, 0.2 us)
Async XLA Ops:
  6.5 186.0 %copy-start = (bf16[512,1024]{1,0:T(8,128)(2,1)S(1)}, bf16[512,1024]{1,0:T(8,128)(2,1)}, u32[]{:S(2)}) copy-start(bf16[512,1024]{1,0:T(8,128)(2,1)} %param.21) | copy-start | bytes 3145732
  17.0 58.6 %copy-start.6 = (bf16[1,1024,2048]{2,1,0:T(8,128)(2,1)S(1)}, bf16[1,1024,2048]{2,1,0:T(8,128)(2,1)}, u32[]{:S(2)}) copy-start(bf16[1,1024,2048]{2,1,0:T(8,128)(2,1)} %param.14) | copy-start | bytes 12582916
  74.2 1.4 copy-start.2
  98.8 4.3 %copy-start.4 = (s32[256,2]{0,1:T(2,128)S(1)}, s32[256,2]{0,1:T(2,128)}, u32[]{:S(2)}) copy-start(s32[256,2]{0,1:T(2,128)} %param.12) | copy-start | bytes 6148
  98.8 4.5 %copy-start.5 = (f32[256,2]{0,1:T(2,128)S(1)}, f32[256,2]{0,1:T(2,128)}, u32[]{:S(2)}) copy-start(f32[256,2]{0,1:T(2,128)} %param.13) | copy-start | bytes 6148
  98.8 46.6 %all-to-all-start.1 = ((bf16[16,64,1024]{2,1,0:T(8,128)(2,1)}), bf16[16,64,1024]{2,1,0:T(8,128)(2,1)S(1)}, u32[]{:S(2)}, u32[]{:S(2)}) async-start(bf16[16,64,1024]{2,1,0:T(8,128)(2,1)} %fusion.14), calls=%async_computation.1 | async-start | bytes 4194304 | tf_op jit(solution)/shard_map/all_to_all | solution.py:66
  102.9 75.0 %all-reduce.2.cloned.1.call-start = ((), (), s32[]{:S(2)}) async-start(), calls=%async_computation.3 | async-start | bytes 1048576 | tf_op jit(solution)/shard_map/psum | solution.py:70
  148.2 10.4 %copy-start.3 = (bf16[31,512]{1,0:T(8,128)(2,1)S(1)}, bf16[31,512]{1,0:T(8,128)(2,1)}, u32[]{:S(2)}) copy-start(bf16[31,512]{1,0:T(8,128)(2,1)} %param.20) | copy-start | bytes 95236
  148.2 29.6 %copy-start.1 = (bf16[256,1024]{1,0:T(8,128)(2,1)S(1)}, bf16[256,1024]{1,0:T(8,128)(2,1)}, u32[]{:S(2)}) copy-start(bf16[256,1024]{1,0:T(8,128)(2,1)} %param.11) | copy-start | bytes 1572868
  154.8 25.7 %copy-start.7 = (f32[1024]{0:T(1024)S(1)}, f32[1024]{0:T(1024)}, u32[]{:S(2)}) copy-start(f32[1024]{0:T(1024)} %param.18) | copy-start | bytes 12292
  154.8 25.7 %copy-start.8 = (f32[1024]{0:T(1024)S(1)}, f32[1024]{0:T(1024)}, u32[]{:S(2)}) copy-start(f32[1024]{0:T(1024)} %param.17) | copy-start | bytes 12292
  154.8 52.5 %reduce-scatter.2.cloned.1.call-start = ((), (), s32[]{:S(2)}) async-start(), calls=%async_computation.4 | async-start | bytes 786432 | tf_op jit(solution)/shard_map/reduce_scatter | solution.py:97
  183.2 5.1 %collective-permute-start = (bf16[15,512]{1,0:T(8,128)(2,1)S(1)}, bf16[15,512]{1,0:T(8,128)(2,1)S(1)}, u32[]{:S(2)}, u32[]{:S(2)}) collective-permute-start(bf16[15,512]{1,0:T(8,128)(2,1)S(1)} %get-tuple-element.7), channel_id=1, source_target_pairs={{0,2},{2,4},{4,6},{6,8},{8,10},{10,12},{12,14},{14,16},{16,18},{18... | collective-permute-start | bytes 46088 | tf_op jit(solution)/shard_map/ppermute | solution.py:15
  186.9 5.6 %collective-permute-start.1 = (bf16[15,512]{1,0:T(8,128)(2,1)S(1)}, bf16[15,512]{1,0:T(8,128)(2,1)S(1)}, u32[]{:S(2)}, u32[]{:S(2)}) collective-permute-start(bf16[15,512]{1,0:T(8,128)(2,1)S(1)} %get-tuple-element.8), channel_id=1, source_target_pairs={{2,0},{4,2},{6,4},{8,6},{10,8},{12,10},{14,12},{16,14},{18,16},{20... | collective-permute-start | bytes 46088 | tf_op jit(solution)/shard_map/ppermute | solution.py:17
Sparse Core Ops, SparseCore 0:
  154.9 22.8 all-reduce.1
  197.6 9.7 reduce-scatter.1
where the time goes:
time: 216 us
  waiting for transfers between devices  75.3 us (35%)
  blocking collectives  57.2 us (26%)
  matrix products  30.7 us (14%)
  local copies, waits for them, and re-layouts  18.2 us (8%)
  between operations  13.6 us (6%)
  other arithmetic  11.6 us (5%)
  starting transfers between devices  9.26 us (4%)
    all_to_all x1, blocking collectives, shards(): lax.all_to_all(outgoing, 'wide', split_axis=0, concat_axis=0, tiled=True)  57.2 us
    all_to_all x1, waiting for transfers between devices, shards(): lax.all_to_all(partial_value, 'wide', split_axis=0, concat_axis=0, tiled=...  41.9 us
    psum x1, waiting for transfers between devices, shards(): lax.psum(mixture.astype(jnp.bfloat16), 'narrow').astype(jnp.float32)  19.2 us
    dot_general x1, matrix products, shards(): jnp.einsum('sjcf,jfd->sjcd', hidden, w_down, preferred_element_type=jnp.f...  16.6 us
    reduce_scatter x1, waiting for transfers between devices, shards(): lax.psum_scatter(jnp.dot(activated, point_out, preferred_element_type=jnp...  9.88 us
    dot_general x1, matrix products, shards(): jnp.einsum('sjcd,jdf->sjcf', arrived, w_gate, preferred_element_type=jnp....  6.63 us
    unnamed x21, local copies, waits for them, and re-layouts  5.97 us
    reduce_sum x1, other arithmetic, shards(): jnp.sum(gate_values[:, :, None] * picked.astype(jnp.float32), axis=1)  5.05 us
  transfers between devices with their start and end apart: 5, of which 5 were waited for; matrix products, arithmetic and copies ran while one was open for 2% of the time, Pallas kernels for 0%

commit v1 on v0

v1 whole, which is shorter than its diff:
```python
import functools

import jax
import jax.numpy as jnp
from jax import lax
from jax.experimental import pallas as pl
from jax.experimental.pallas import tpu as pltpu
from jax.sharding import PartitionSpec as P

F32 = jnp.float32
BF16 = jnp.bfloat16
HALO = 16


def block_kernel(
    wide,
    narrow,
    groups,
    cap,
    frames_ref,
    ids_ref,
    gates_ref,
    gain_ref,
    bias_ref,
    depth_ref,
    w_gate_hbm,
    w_up_hbm,
    w_down_hbm,
    pin_hbm,
    pout_hbm,
    out_ref,
    w_gate,
    w_up,
    w_down,
    pin,
    pout,
    outgoing,
    arrived,
    hidden,
    partial,
    partial_in,
    sums,
    returned,
    mix0,
    mix1,
    mixed,
    residual,
    padded,
    padded32,
    activated,
    shares,
    shares_in,
    w_sem,
    fs,
    fr,
    xs,
    xr,
    ps,
    pr,
    rs,
    rr,
    ms,
    mr,
    hs,
    hr,
    os_,
    or_,
):
    me_w = lax.axis_index("wide")
    me_n = lax.axis_index("narrow")
    frame_count, width = frames_ref.shape
    dc = width // narrow
    size = wide // groups
    rows = size * cap
    plane = me_w // size
    inner = me_w % size
    units = w_gate.shape[1]
    channels = pout.shape[0]
    share = frame_count // narrow
    taps = depth_ref.shape[0]

    def cols(index):
        return pl.ds(pl.multiple_of(index * dc, 128), dc)

    def slots(index):
        return pl.ds(pl.multiple_of(index * cap, 16), cap)

    def group_rows(index):
        return pl.ds(pl.multiple_of(index * rows, 16), rows)

    def share_rows(index):
        return pl.ds(pl.multiple_of(index * share, 16), share)

    my_cols = cols(me_n)

    barrier = pltpu.get_barrier_semaphore()

    def greet(i, carry):
        pl.semaphore_signal(
            barrier,
            inc=1,
            device_id=((me_w + i) % wide, me_n),
            device_id_type=pl.DeviceIdType.MESH,
        )
        return carry

    lax.fori_loop(1, wide, greet, 0)
    for i in range(1, narrow):
        pl.semaphore_signal(
            barrier,
            inc=1,
            device_id=(me_w, (me_n + i) % narrow),
            device_id_type=pl.DeviceIdType.MESH,
        )

    loads = [
        pltpu.make_async_copy(w_gate_hbm.at[0], w_gate, w_sem.at[0]),
        pltpu.make_async_copy(w_up_hbm.at[0], w_up, w_sem.at[1]),
        pltpu.make_async_copy(w_down_hbm.at[0], w_down, w_sem.at[2]),
        pltpu.make_async_copy(pin_hbm, pin, w_sem.at[3]),
        pltpu.make_async_copy(pout_hbm, pout, w_sem.at[4]),
    ]
    for load in loads:
        load.start()

    def remote(src, dst, send, recv, device):
        return pltpu.make_async_remote_copy(
            src_ref=src,
            dst_ref=dst,
            send_sem=send,
            recv_sem=recv,
            device_id=device,
            device_id_type=pl.DeviceIdType.MESH,
        )

    id0 = ids_ref[:, 0:1]
    id1 = ids_ref[:, 1:2]
    lane = lax.broadcasted_iota(jnp.int32, (frame_count, 128), 1)
    named0 = lane == id0
    named1 = lane == id1
    named = jnp.where(named0 | named1, 1.0, 0.0).astype(BF16)
    earlier = jnp.where(
        lax.broadcasted_iota(jnp.int32, (frame_count, frame_count), 0)
        > lax.broadcasted_iota(jnp.int32, (frame_count, frame_count), 1),
        1.0,
        0.0,
    ).astype(BF16)
    position = jnp.dot(earlier, named, preferred_element_type=F32)
    slot0 = id0.astype(F32) * cap + jnp.sum(
        jnp.where(named0, position, 0.0), axis=1, keepdims=True
    )
    slot1 = id1.astype(F32) * cap + jnp.sum(
        jnp.where(named1, position, 0.0), axis=1, keepdims=True
    )
    both = jnp.where(lane == 0, slot0, jnp.where(lane == 1, slot1, 0.0))
    turned = jnp.transpose(both).astype(jnp.int32)
    row0 = turned[0:1, :]
    row1 = turned[1:2, :]
    slot0 = slot0.astype(jnp.int32)
    slot1 = slot1.astype(jnp.int32)

    def send_copy(p):
        return remote(
            outgoing.at[slots(p), :],
            arrived.at[slots(me_w), my_cols],
            fs.at[p],
            fr.at[me_w],
            (p, me_n),
        )

    def recv_copy(s):
        return remote(
            outgoing.at[slots(s), :],
            arrived.at[slots(s), my_cols],
            fs.at[s],
            fr.at[s],
            (s, me_n),
        )

    mine = frames_ref[:, my_cols]
    for g in range(groups):
        q = (plane + g) % groups
        place = lax.broadcasted_iota(jnp.int32, (rows, frame_count), 0) + q * rows
        choose = jnp.where((place == row0) | (place == row1), 1.0, 0.0).astype(BF16)
        outgoing[group_rows(q), :] = jnp.dot(
            choose, mine, preferred_element_type=F32
        ).astype(BF16)
        if g == 0:
            arrived[slots(me_w), my_cols] = outgoing[slots(me_w), :]
            pl.semaphore_wait(barrier, wide - 1 + narrow - 1)

        def send(i, carry, q=q):
            send_copy(q * size + (inner + i) % size).start()
            return carry

        lax.fori_loop(1 if g == 0 else 0, size, send, 0)

    def forward_copy(g, q, m):
        part = arrived.at[group_rows(q), my_cols]
        return remote(part, part, xs.at[g, m], xr.at[g, me_n], (me_w, m))

    def forward_in(g, q, m):
        part = arrived.at[group_rows(q), cols(m)]
        return remote(part, part, xs.at[g, m], xr.at[g, m], (me_w, m))

    def partial_copy(g, q, m):
        return remote(
            partial.at[group_rows(q), cols(m)],
            partial_in.at[me_n, group_rows(q), :],
            ps.at[g, m],
            pr.at[g, me_n],
            (me_w, m),
        )

    def partial_wait(g, q, m):
        return remote(
            partial.at[group_rows(q), cols(m)],
            partial_in.at[m, group_rows(q), :],
            ps.at[g, m],
            pr.at[g, m],
            (me_w, m),
        )

    def return_copy(s):
        return remote(
            sums.at[slots(s), :],
            returned.at[slots(me_w), :],
            rs.at[s],
            rr.at[me_w],
            (s, me_n),
        )

    def return_wait(p):
        return remote(
            sums.at[slots(p), :],
            returned.at[slots(p), :],
            rs.at[p],
            rr.at[p],
            (p, me_n),
        )

    siblings = [(me_n + i) % narrow for i in range(1, narrow)]
    tile = min(512, units)

    def step(g, carry):
        q = (plane + groups - g) % groups

        def take(i, c):
            s = q * size + (inner + size - i) % size

            @pl.when(s != me_w)
            def _():
                recv_copy(s).wait_recv()

            return c

        lax.fori_loop(0, size, take, 0)
        for m in siblings:
            forward_copy(g, q, m).start()

        @pl.when(g == 0)
        def _():
            for load in loads[:3]:
                load.wait()

        for m in siblings:
            forward_in(g, q, m).wait_recv()

        x = arrived[group_rows(q), :]
        for f in range(0, units, tile):
            gate = jnp.dot(x, w_gate[:, f : f + tile], preferred_element_type=F32)
            up = jnp.dot(x, w_up[:, f : f + tile], preferred_element_type=F32)
            hidden[:, f : f + tile] = (gate * jax.nn.sigmoid(gate) * up).astype(BF16)
        for m in siblings:
            partial[group_rows(q), cols(m)] = jnp.dot(
                hidden[...], w_down[:, cols(m)], preferred_element_type=F32
            ).astype(BF16)
            partial_copy(g, q, m).start()
        total = jnp.dot(hidden[...], w_down[:, my_cols], preferred_element_type=F32)
        for m in siblings:
            partial_wait(g, q, m).wait_recv()
            total = total + partial_in[m, group_rows(q), :].astype(F32)
        sums[group_rows(q), :] = total.astype(BF16)

        def give(i, c):
            s = q * size + (inner + size - i) % size

            @pl.when(s != me_w)
            def _():
                return_copy(s).start()

            return c

        lax.fori_loop(0, size, give, 0)
        return carry

    lax.fori_loop(0, groups, step, 0)
    returned[slots(me_w), :] = sums[slots(me_w), :]

    mix0[...] = jnp.zeros_like(mix0)
    mix1[...] = jnp.zeros_like(mix1)

    def combine(g, carry):
        q = (plane + g) % groups

        def take(i, c):
            p = q * size + (inner + i) % size

            @pl.when(p != me_w)
            def _():
                return_wait(p).wait_recv()

            return c

        lax.fori_loop(0, size, take, 0)
        place = lax.broadcasted_iota(jnp.int32, (frame_count, rows), 1) + q * rows
        block = returned[group_rows(q), :]
        mix0[...] += jnp.dot(
            jnp.where(place == slot0, 1.0, 0.0).astype(BF16), block, preferred_element_type=F32
        )
        mix1[...] += jnp.dot(
            jnp.where(place == slot1, 1.0, 0.0).astype(BF16), block, preferred_element_type=F32
        )
        return carry

    lax.fori_loop(0, groups, combine, 0)
    mixed[:, my_cols] = (
        gates_ref[:, 0:1] * mix0[...] + gates_ref[:, 1:2] * mix1[...]
    ).astype(BF16)

    def mix_copy(m):
        part = mixed.at[:, my_cols]
        return remote(part, part, ms.at[m], mr.at[me_n], (me_w, m))

    def mix_wait(m):
        part = mixed.at[:, cols(m)]
        return remote(part, part, ms.at[m], mr.at[m], (me_w, m))

    for m in siblings:
        mix_copy(m).start()
    for load in loads[3:]:
        load.wait()
    for m in siblings:
        mix_wait(m).wait_recv()

    res = frames_ref[...].astype(F32) + mixed[...].astype(F32)
    residual[...] = res
    centered = res - jnp.mean(res, axis=1, keepdims=True)
    variance = jnp.mean(centered * centered, axis=1, keepdims=True)
    normed = (centered * lax.rsqrt(variance + 1e-05) * gain_ref[...] + bias_ref[...]).astype(BF16)
    value_half = jnp.dot(normed, pin[:, :channels], preferred_element_type=F32)
    gate_half = jnp.dot(normed, pin[:, channels:], preferred_element_type=F32)
    glu = (value_half * jax.nn.sigmoid(gate_half)).astype(BF16)
    padded[HALO : HALO + frame_count, :] = glu
    padded32[HALO : HALO + frame_count, :] = glu.astype(F32)

    end = HALO + frame_count
    to_left = remote(
        padded.at[HALO : 2 * HALO, :],
        padded.at[end : end + HALO, :],
        hs.at[0],
        hr.at[0],
        ((me_w + wide - 1) % wide, me_n),
    )
    to_right = remote(
        padded.at[frame_count:end, :],
        padded.at[0:HALO, :],
        hs.at[1],
        hr.at[1],
        ((me_w + 1) % wide, me_n),
    )
    has_left = me_w > 0
    has_right = me_w < wide - 1

    @pl.when(has_left)
    def _():
        to_left.start()

    @pl.when(has_right)
    def _():
        to_right.start()

    half = (taps - 1) // 2
    step_rows = 64

    def depthwise(starts):
        def strip(c, carry):
            lanes = pl.ds(pl.multiple_of(c * 128, 128), 128)
            kernel_taps = depth_ref[:, lanes].astype(F32)
            for start in starts:
                total = jnp.zeros((step_rows, 128), F32)
                for j in range(taps):
                    low = start + HALO - half + j
                    total = total + padded32[low : low + step_rows, lanes] * kernel_taps[j : j + 1, :]
                activated[start : start + step_rows, lanes] = (
                    total * jax.nn.sigmoid(total)
                ).astype(BF16)
            return carry

        lax.fori_loop(0, channels // 128, strip, 0)

    depthwise(range(step_rows, frame_count - step_rows, step_rows))

    @pl.when(has_right)
    def _():
        to_left.wait_recv()
        padded32[end : end + HALO, :] = padded[end : end + HALO, :].astype(F32)

    @pl.when(jnp.logical_not(has_right))
    def _():
        padded32[end : end + HALO, :] = jnp.zeros((HALO, channels), F32)

    @pl.when(has_left)
    def _():
        to_right.wait_recv()
        padded32[0:HALO, :] = padded[0:HALO, :].astype(F32)

    @pl.when(jnp.logical_not(has_left))
    def _():
        padded32[0:HALO, :] = jnp.zeros((HALO, channels), F32)

    depthwise((0, frame_count - step_rows))

    def share_copy(m):
        return remote(
            shares.at[share_rows(m), :], shares_in.at[me_n], os_.at[m], or_.at[me_n], (me_w, m)
        )

    def share_wait(m):
        return remote(
            shares.at[share_rows(m), :], shares_in.at[m], os_.at[m], or_.at[m], (me_w, m)
        )

    for m in siblings:
        shares[share_rows(m), :] = jnp.dot(
            activated[share_rows(m), :], pout[...], preferred_element_type=F32
        ).astype(BF16)
        share_copy(m).start()
    total = residual[share_rows(me_n), :] + jnp.dot(
        activated[share_rows(me_n), :], pout[...], preferred_element_type=F32
    )
    for m in siblings:
        share_wait(m).wait_recv()
        total = total + shares_in[m].astype(F32)
    out_ref[...] = total.astype(BF16)

    def finish(i, carry):
        p = (me_w + i) % wide
        send_copy(p).wait_send()
        return_copy(p).wait_send()
        return carry

    lax.fori_loop(1, wide, finish, 0)
    for m in siblings:
        mix_copy(m).wait_send()
        share_copy(m).wait_send()

    def finish_group(g, carry):
        q = (plane + groups - g) % groups
        for m in siblings:
            forward_copy(g, q, m).wait_send()
            partial_copy(g, q, m).wait_send()
        return carry

    lax.fori_loop(0, groups, finish_group, 0)

    @pl.when(has_left)
    def _():
        to_left.wait_send()

    @pl.when(has_right)
    def _():
        to_right.wait_send()


def shards(
    frames,
    expert_ids,
    gate_values,
    w_gate,
    w_up,
    w_down,
    norm_gain,
    norm_bias,
    point_in,
    depth_kernel,
    point_out,
):
    frame_count, width = frames.shape
    top_count = expert_ids.shape[1]
    wide = lax.axis_size("wide")
    narrow = lax.axis_size("narrow")
    expert_count = w_gate.shape[0] * wide
    cap = 2 * top_count * frame_count // expert_count
    units = w_gate.shape[2]
    channels = point_in.shape[2]
    groups = 4
    slot_count = wide * cap
    rows = slot_count // groups
    dc = width // narrow
    share = frame_count // narrow
    vmem = pl.BlockSpec(memory_space=pltpu.VMEM)
    hbm = pl.BlockSpec(memory_space=pl.ANY)
    dma = pltpu.SemaphoreType.DMA
    flops = 2 * width * (3 * slot_count * units + 3 * frame_count * channels)
    return pl.pallas_call(
        functools.partial(block_kernel, wide, narrow, groups, cap),
        out_shape=jax.ShapeDtypeStruct((share, width), BF16),
        in_specs=[vmem] * 6 + [hbm] * 5,
        out_specs=vmem,
        scratch_shapes=[
            pltpu.VMEM((width, units), BF16),
            pltpu.VMEM((width, units), BF16),
            pltpu.VMEM((units, width), BF16),
            pltpu.VMEM((width, 2 * channels), BF16),
            pltpu.VMEM((channels, width), BF16),
            pltpu.VMEM((slot_count, dc), BF16),
            pltpu.VMEM((slot_count, width), BF16),
            pltpu.VMEM((rows, units), BF16),
            pltpu.VMEM((slot_count, width), BF16),
            pltpu.VMEM((narrow, slot_count, dc), BF16),
            pltpu.VMEM((slot_count, dc), BF16),
            pltpu.VMEM((slot_count, dc), BF16),
            pltpu.VMEM((frame_count, dc), F32),
            pltpu.VMEM((frame_count, dc), F32),
            pltpu.VMEM((frame_count, width), BF16),
            pltpu.VMEM((frame_count, width), F32),
            pltpu.VMEM((frame_count + 2 * HALO, channels), BF16),
            pltpu.VMEM((frame_count + 2 * HALO, channels), F32),
            pltpu.VMEM((frame_count, channels), BF16),
            pltpu.VMEM((frame_count, width), BF16),
            pltpu.VMEM((narrow, share, width), BF16),
            dma((5,)),
            dma((wide,)),
            dma((wide,)),
            dma((groups, narrow)),
            dma((groups, narrow)),
            dma((groups, narrow)),
            dma((groups, narrow)),
            dma((wide,)),
            dma((wide,)),
            dma((narrow,)),
            dma((narrow,)),
            dma((2,)),
            dma((2,)),
            dma((narrow,)),
            dma((narrow,)),
        ],
        compiler_params=pltpu.CompilerParams(
            collective_id=0, has_side_effects=True, vmem_limit_bytes=56 * 1024 * 1024
        ),
        cost_estimate=pl.CostEstimate(
            flops=flops, bytes_accessed=2 * 3 * width * units, transcendentals=0
        ),
        name="conformer_block",
    )(
        frames,
        expert_ids,
        gate_values,
        norm_gain.reshape(1, width),
        norm_bias.reshape(1, width),
        depth_kernel,
        w_gate,
        w_up,
        w_down,
        point_in.reshape(width, 2 * channels),
        point_out,
    )


def solution(mesh):
    return jax.shard_map(
        shards,
        mesh=mesh,
        in_specs=(
            P("wide", None),
            P("wide", None),
            P("wide", None),
            P("wide", None, "narrow"),
            P("wide", None, "narrow"),
            P("wide", "narrow", None),
            P(),
            P(),
            P(None, None, "narrow"),
            P(None, "narrow"),
            P("narrow", None),
        ),
        out_specs=P(("wide", "narrow"), None),
        check_vma=False,
    )
```

time: 216 us -> 84.4 us (0.39)
  Pallas kernels: 0 us -> 76 us
  waiting for transfers between devices: 75.3 us -> 0 us
  blocking collectives: 57.2 us -> 0 us
  matrix products: 30.7 us -> 0 us
  between operations: 13.6 us -> 0.01 us
  other arithmetic: 11.6 us -> 0 us
  local copies, waits for them, and re-layouts: 18.2 us -> 8.12 us
  starting transfers between devices: 9.26 us -> 0 us
    pallas_call x0 -> x1, Pallas kernels: none -> 76 us  [shards(): pl.pallas_call(functools.partial(block_kernel, wide, narrow, groups, cap)...]
    all_to_all x1 -> x0, blocking collectives: 57.2 us -> none  [shards(): lax.all_to_all(outgoing, 'wide', split_axis=0, concat_axis=0, tiled=True)]
    all_to_all x1 -> x0, waiting for transfers between devices: 41.9 us -> none  [shards(): lax.all_to_all(partial_value, 'wide', split_axis=0, concat_axis=0, tiled=...]
    dot_general x4 -> x0, matrix products: 30.7 us -> none  [the longest x1 16.6 us: shards(): jnp.einsum('sjcf,jfd->sjcd', hidden, w_down, preferred_element_type=jnp.f...]
    psum x1 -> x0, waiting for transfers between devices: 19.2 us -> none  [shards(): lax.psum(mixture.astype(jnp.bfloat16), 'narrow').astype(jnp.float32)]
    reduce_scatter x1 -> x0, waiting for transfers between devices: 9.88 us -> none  [shards(): lax.psum_scatter(jnp.dot(activated, point_out, preferred_element_type=jnp...]
    reduce_sum x3 -> x0, other arithmetic: 6.48 us -> none  [the longest x1 5.05 us: shards(): jnp.sum(gate_values[:, :, None] * picked.astype(jnp.float32), axis=1)]
    ppermute x2 -> x0, starting transfers between devices: 4.94 us -> none  [the longest x1 3.64 us: padded_2(): lax.ppermute(tail, axis, [(i, (i + 1) % count) for i in range(ends)])]
  transfers between devices with their start and end apart: 5 -> 0, of which waited for: 5 -> 0; matrix products, arithmetic and copies ran while one was open for 2% -> 0% of each run, Pallas kernels for 0% -> 0%
where the time goes in v1:
time: 84.4 us; the launch traced here: 84.1 us
  Pallas kernels  76 us (90%)
  local copies, waits for them, and re-layouts  8.12 us (10%)
    pallas_call x1, Pallas kernels, shards(): pl.pallas_call(functools.partial(block_kernel, wide, narrow, groups, cap)...  76 us
    unnamed x4, local copies, waits for them, and re-layouts  8.12 us

profile of v1, /device:TPU:0, one launch (start us, length us, event | category | flops | bytes accessed | tf_op | source)
XLA Modules:
  0.0 84.1 jit_solution(16894195917199731378)
XLA Ops:
  0.0 1.5 %copy.12.ids_ref = s32[256,2]{1,0:T(8,128)} copy(s32[256,2]{0,1:T(2,128)} %param.12) | data formatting | bytes 4096 | tf_op args[1]
  1.5 1.5 %copy.13.gates_ref = f32[256,2]{1,0:T(8,128)} copy(f32[256,2]{0,1:T(2,128)} %param.13) | data formatting | bytes 4096 | tf_op args[2]
  2.9 3.5 %copy.14 = bf16[128,8,2,512]{3,1,2,0:T(8,128)(2,1)} copy(bf16[128,8,2,512]{3,2,1,0:T(2,128)(2,1)} %bitcast.4) | data formatting | bytes 4194304
  6.5 76.0 %conformer_block.1 = bf16[128,1024]{1,0:T(8,128)(2,1)} custom-call(bf16[256,1024]{1,0:T(8,128)(2,1)} %frames_ref.1, s32[256,2]{1,0:T(8,128)} %copy.12.ids_ref, f32[256,2]{1,0:T(8,128)} %copy.13.gates_ref, f32[1,1024]{1,0:T(1,128)} %bitcast.6, f32[1,1024]{1,0:T(1,128)} %bitcast.7, bf16[31,512]{1,0:T(8,128)(2,1)} %depth_ref.1, ...), custom_call_target="tpu_custom_call" | custom-call | flops 13690208256 | bytes 12582912 | tf_op jit(solution)/shard_map/conformer_block/pallas_call | solution.py:506
  82.4 1.7 %copy.16 = bf16[128,1024]{1,0:T(8,128)(2,1)} copy(bf16[128,1024]{1,0:T(8,128)(2,1)} %conformer_block.1) | data formatting | bytes 524288

commit v2 on v1

--- a/solution.py
+++ b/solution.py
@@ -32,8 +32,10 @@
     w_gate,
     w_up,
     w_down,
+    pin_raw,
     pin,
     pout,
+    turned,
     outgoing,
     arrived,
     hidden,
@@ -117,7 +119,7 @@
         pltpu.make_async_copy(w_gate_hbm.at[0], w_gate, w_sem.at[0]),
         pltpu.make_async_copy(w_up_hbm.at[0], w_up, w_sem.at[1]),
         pltpu.make_async_copy(w_down_hbm.at[0], w_down, w_sem.at[2]),
-        pltpu.make_async_copy(pin_hbm, pin, w_sem.at[3]),
+        pltpu.make_async_copy(pin_hbm, pin_raw, w_sem.at[3]),
         pltpu.make_async_copy(pout_hbm, pout, w_sem.at[4]),
     ]
     for load in loads:
@@ -133,31 +135,38 @@
             device_id_type=pl.DeviceIdType.MESH,
         )
 
-    id0 = ids_ref[:, 0:1]
-    id1 = ids_ref[:, 1:2]
-    lane = lax.broadcasted_iota(jnp.int32, (frame_count, 128), 1)
+    id0 = ids_ref[0:1, :]
+    id1 = ids_ref[1:2, :]
+    lane = lax.broadcasted_iota(jnp.int32, (128, frame_count), 0)
     named0 = lane == id0
     named1 = lane == id1
     named = jnp.where(named0 | named1, 1.0, 0.0).astype(BF16)
     earlier = jnp.where(
         lax.broadcasted_iota(jnp.int32, (frame_count, frame_count), 0)
-        > lax.broadcasted_iota(jnp.int32, (frame_count, frame_count), 1),
+        < lax.broadcasted_iota(jnp.int32, (frame_count, frame_count), 1),
         1.0,
         0.0,
     ).astype(BF16)
-    position = jnp.dot(earlier, named, preferred_element_type=F32)
-    slot0 = id0.astype(F32) * cap + jnp.sum(
-        jnp.where(named0, position, 0.0), axis=1, keepdims=True
-    )
-    slot1 = id1.astype(F32) * cap + jnp.sum(
-        jnp.where(named1, position, 0.0), axis=1, keepdims=True
-    )
-    both = jnp.where(lane == 0, slot0, jnp.where(lane == 1, slot1, 0.0))
-    turned = jnp.transpose(both).astype(jnp.int32)
-    row0 = turned[0:1, :]
-    row1 = turned[1:2, :]
-    slot0 = slot0.astype(jnp.int32)
-    slot1 = slot1.astype(jnp.int32)
+    position = jnp.dot(named, earlier, preferred_element_type=F32)
+    row0 = id0.astype(F32) * cap + jnp.sum(
+        jnp.where(named0, position, 0.0), axis=0, keepdims=True
+    )
+    row1 = id1.astype(F32) * cap + jnp.sum(
+        jnp.where(named1, position, 0.0), axis=0, keepdims=True
+    )
+    stacked = jnp.where(
+        lane == 0,
+        row0,
+        jnp.where(
+            lane == 1, row1, jnp.where(lane == 2, gates_ref[0:1, :], gates_ref[1:2, :])
+        ),
+    )
+    turned[...] = jnp.transpose(stacked)
+    row0 = row0.astype(jnp.int32)
+    row1 = row1.astype(jnp.int32)
+
+    def plane_of(g):
+        return ((plane // 2 + g % 2) % 2) * 2 + (plane % 2 + g // 2) % 2
 
     def send_copy(p):
         return remote(
@@ -178,16 +187,17 @@
         )
 
     mine = frames_ref[:, my_cols]
-    for g in range(groups):
-        q = (plane + g) % groups
+    for turn, g in enumerate((1, 0, 3, 2)):
+        q = plane_of(g)
         place = lax.broadcasted_iota(jnp.int32, (rows, frame_count), 0) + q * rows
         choose = jnp.where((place == row0) | (place == row1), 1.0, 0.0).astype(BF16)
         outgoing[group_rows(q), :] = jnp.dot(
             choose, mine, preferred_element_type=F32
         ).astype(BF16)
+        if turn == 0:
+            pl.semaphore_wait(barrier, wide - 1 + narrow - 1)
         if g == 0:
             arrived[slots(me_w), my_cols] = outgoing[slots(me_w), :]
-            pl.semaphore_wait(barrier, wide - 1 + narrow - 1)
 
         def send(i, carry, q=q):
             send_copy(q * size + (inner + i) % size).start()
@@ -243,7 +253,20 @@
     tile = min(512, units)
 
     def step(g, carry):
-        q = (plane + groups - g) % groups
+        q = plane_of(g)
+
+        @pl.when(g == 1)
+        def _():
+            for load in loads[3:]:
+                load.wait()
+
+            def sort(i, c):
+                r = pl.ds(pl.multiple_of(i * 64, 64), 64)
+                pin[r, :channels] = pin_raw[r, 0, :]
+                pin[r, channels:] = pin_raw[r, 1, :]
+                return c
+
+            lax.fori_loop(0, width // 64, sort, 0)
 
         def take(i, c):
             s = q * size + (inner + size - i) % size
@@ -301,7 +324,7 @@
     mix1[...] = jnp.zeros_like(mix1)
 
     def combine(g, carry):
-        q = (plane + g) % groups
+        q = plane_of(g)
 
         def take(i, c):
             p = q * size + (inner + i) % size
@@ -316,16 +339,16 @@
         place = lax.broadcasted_iota(jnp.int32, (frame_count, rows), 1) + q * rows
         block = returned[group_rows(q), :]
         mix0[...] += jnp.dot(
-            jnp.where(place == slot0, 1.0, 0.0).astype(BF16), block, preferred_element_type=F32
+            jnp.where(place == turned[:, 0:1].astype(jnp.int32), 1.0, 0.0).astype(BF16), block, preferred_element_type=F32
         )
         mix1[...] += jnp.dot(
-            jnp.where(place == slot1, 1.0, 0.0).astype(BF16), block, preferred_element_type=F32
+            jnp.where(place == turned[:, 1:2].astype(jnp.int32), 1.0, 0.0).astype(BF16), block, preferred_element_type=F32
         )
         return carry
 
     lax.fori_loop(0, groups, combine, 0)
     mixed[:, my_cols] = (
-        gates_ref[:, 0:1] * mix0[...] + gates_ref[:, 1:2] * mix1[...]
+        turned[:, 2:3] * mix0[...] + turned[:, 3:4] * mix1[...]
     ).astype(BF16)
 
     def mix_copy(m):
@@ -338,8 +361,6 @@
 
     for m in siblings:
         mix_copy(m).start()
-    for load in loads[3:]:
-        load.wait()
     for m in siblings:
         mix_wait(m).wait_recv()
 
@@ -456,7 +477,7 @@
         share_copy(m).wait_send()
 
     def finish_group(g, carry):
-        q = (plane + groups - g) % groups
+        q = plane_of(g)
         for m in siblings:
             forward_copy(g, q, m).wait_send()
             partial_copy(g, q, m).wait_send()
@@ -512,8 +533,10 @@
             pltpu.VMEM((width, units), BF16),
             pltpu.VMEM((width, units), BF16),
             pltpu.VMEM((units, width), BF16),
+            pltpu.VMEM((width, 2, channels), BF16),
             pltpu.VMEM((width, 2 * channels), BF16),
             pltpu.VMEM((channels, width), BF16),
+            pltpu.VMEM((frame_count, 128), F32),
             pltpu.VMEM((slot_count, dc), BF16),
             pltpu.VMEM((slot_count, width), BF16),
             pltpu.VMEM((rows, units), BF16),
@@ -555,15 +578,15 @@
         name="conformer_block",
     )(
         frames,
-        expert_ids,
-        gate_values,
+        expert_ids.T,
+        gate_values.T,
         norm_gain.reshape(1, width),
         norm_bias.reshape(1, width),
         depth_kernel,
         w_gate,
         w_up,
         w_down,
-        point_in.reshape(width, 2 * channels),
+        point_in,
         point_out,
     )
 

time: 84.4 us -> 68.4 us (0.81)
  the two profiles are of different devices: /device:TPU:0 before, /device:TPU:25 now
where the time goes in v2:
time: 68.4 us; the launch traced here: 68.3 us
  Pallas kernels  66.6 us (97%)
  local copies, waits for them, and re-layouts  1.67 us (2%)
    pallas_call x1, Pallas kernels, shards(): pl.pallas_call(functools.partial(block_kernel, wide, narrow, groups, cap)...  66.6 us
    unnamed x1, local copies, waits for them, and re-layouts  1.67 us

profile of v2, /device:TPU:25, one launch (start us, length us, event | category | flops | bytes accessed | tf_op | source)
XLA Modules:
  0.0 68.3 jit_solution(18012302469179108792)
XLA Ops:
  0.0 66.6 %conformer_block.1 = bf16[128,1024]{1,0:T(8,128)(2,1)} custom-call(bf16[256,1024]{1,0:T(8,128)(2,1)} %frames_ref.1, s32[2,256]{1,0:T(2,128)} %bitcast.6, f32[2,256]{1,0:T(2,128)} %bitcast.7, f32[1,1024]{1,0:T(1,128)} %bitcast.4, f32[1,1024]{1,0:T(1,128)} %bitcast.5, bf16[31,512]{1,0:T(8,128)(2,1)} %depth_ref.1, bf16[1,1024,2048]{2,1,0:T(8,128)(2,1)} %w_gate_hbm.1, ...), custom_call_target="tpu_custom_call" | custom-call | flops 13690208256 | bytes 12582912 | tf_op jit(solution)/shard_map/conformer_block/pallas_call | solution.py:527
  66.6 1.7 %copy.13 = bf16[128,1024]{1,0:T(8,128)(2,1)} copy(bf16[128,1024]{1,0:T(8,128)(2,1)} %conformer_block.1) | data formatting | bytes 524288

commit v3 on v2

--- a/solution.py
+++ b/solution.py
@@ -50,8 +50,7 @@
     padded,
     padded32,
     activated,
-    shares,
-    shares_in,
+    taps_all,
     w_sem,
     fs,
     fr,
@@ -67,6 +66,10 @@
     hr,
     os_,
     or_,
+    vs,
+    vr,
+    ts,
+    tr,
 ):
     me_w = lax.axis_index("wide")
     me_n = lax.axis_index("narrow")
@@ -77,9 +80,13 @@
     plane = me_w // size
     inner = me_w % size
     units = w_gate.shape[1]
-    channels = pout.shape[0]
+    channels = pout.shape[0] // narrow
     share = frame_count // narrow
     taps = depth_ref.shape[0]
+    total_count = wide * narrow
+    place_now = me_w * narrow + me_n
+    before = (place_now + total_count - 1) % total_count
+    after = (place_now + 1) % total_count
 
     def cols(index):
         return pl.ds(pl.multiple_of(index * dc, 128), dc)
@@ -115,12 +122,22 @@
             device_id_type=pl.DeviceIdType.MESH,
         )
 
+    for other in (before, after):
+        pl.semaphore_signal(
+            barrier,
+            inc=1,
+            device_id=(other // narrow, other % narrow),
+            device_id_type=pl.DeviceIdType.MESH,
+        )
+
+    own_channels = pl.ds(pl.multiple_of(me_n * channels, 128), channels)
+
     loads = [
         pltpu.make_async_copy(w_gate_hbm.at[0], w_gate, w_sem.at[0]),
         pltpu.make_async_copy(w_up_hbm.at[0], w_up, w_sem.at[1]),
         pltpu.make_async_copy(w_down_hbm.at[0], w_down, w_sem.at[2]),
         pltpu.make_async_copy(pin_hbm, pin_raw, w_sem.at[3]),
-        pltpu.make_async_copy(pout_hbm, pout, w_sem.at[4]),
+        pltpu.make_async_copy(pout_hbm, pout.at[own_channels, :], w_sem.at[4]),
     ]
     for load in loads:
         load.start()
@@ -195,7 +212,7 @@
             choose, mine, preferred_element_type=F32
         ).astype(BF16)
         if turn == 0:
-            pl.semaphore_wait(barrier, wide - 1 + narrow - 1)
+            pl.semaphore_wait(barrier, wide - 1 + narrow - 1 + 2)
         if g == 0:
             arrived[slots(me_w), my_cols] = outgoing[slots(me_w), :]
 
@@ -249,6 +266,26 @@
             (p, me_n),
         )
 
+    def weight_copies(m):
+        taps_part = taps_all.at[me_n]
+        pin_part = pin.at[me_n]
+        pout_part = pout.at[own_channels, :]
+        return (
+            remote(taps_part, taps_part, ts.at[m], tr.at[me_n], (me_w, m)),
+            remote(pin_part, pin_part, vs.at[m], vr.at[me_n], (me_w, m)),
+            remote(pout_part, pout_part, os_.at[m], or_.at[me_n], (me_w, m)),
+        )
+
+    def weight_waits(m):
+        taps_part = taps_all.at[m]
+        pin_part = pin.at[m]
+        pout_part = pout.at[pl.ds(pl.multiple_of(m * channels, 128), channels), :]
+        return (
+            remote(taps_part, taps_part, ts.at[m], tr.at[m], (me_w, m)),
+            remote(pin_part, pin_part, vs.at[m], vr.at[m], (me_w, m)),
+            remote(pout_part, pout_part, os_.at[m], or_.at[m], (me_w, m)),
+        )
+
     siblings = [(me_n + i) % narrow for i in range(1, narrow)]
     tile = min(512, units)
 
@@ -262,11 +299,16 @@
 
             def sort(i, c):
                 r = pl.ds(pl.multiple_of(i * 64, 64), 64)
-                pin[r, :channels] = pin_raw[r, 0, :]
-                pin[r, channels:] = pin_raw[r, 1, :]
+                pin[me_n, r, :channels] = pin_raw[r, 0, :]
+                pin[me_n, r, channels:] = pin_raw[r, 1, :]
                 return c
 
             lax.fori_loop(0, width // 64, sort, 0)
+            taps_all[me_n] = jnp.zeros(taps_all.shape[1:], F32)
+            taps_all[me_n, 0:taps, :] = depth_ref[...].astype(F32)
+            for m in siblings:
+                for copy in weight_copies(m):
+                    copy.start()
 
         def take(i, c):
             s = q * size + (inner + size - i) % size
@@ -351,47 +393,53 @@
         turned[:, 2:3] * mix0[...] + turned[:, 3:4] * mix1[...]
     ).astype(BF16)
 
+    own_rows = share_rows(me_n)
+
     def mix_copy(m):
-        part = mixed.at[:, my_cols]
+        part = mixed.at[share_rows(m), my_cols]
         return remote(part, part, ms.at[m], mr.at[me_n], (me_w, m))
 
     def mix_wait(m):
-        part = mixed.at[:, cols(m)]
+        part = mixed.at[own_rows, cols(m)]
         return remote(part, part, ms.at[m], mr.at[m], (me_w, m))
 
     for m in siblings:
         mix_copy(m).start()
     for m in siblings:
+        for copy in weight_waits(m):
+            copy.wait_recv()
+    for m in siblings:
         mix_wait(m).wait_recv()
 
-    res = frames_ref[...].astype(F32) + mixed[...].astype(F32)
+    res = frames_ref[own_rows, :].astype(F32) + mixed[own_rows, :].astype(F32)
     residual[...] = res
     centered = res - jnp.mean(res, axis=1, keepdims=True)
     variance = jnp.mean(centered * centered, axis=1, keepdims=True)
     normed = (centered * lax.rsqrt(variance + 1e-05) * gain_ref[...] + bias_ref[...]).astype(BF16)
-    value_half = jnp.dot(normed, pin[:, :channels], preferred_element_type=F32)
-    gate_half = jnp.dot(normed, pin[:, channels:], preferred_element_type=F32)
-    glu = (value_half * jax.nn.sigmoid(gate_half)).astype(BF16)
-    padded[HALO : HALO + frame_count, :] = glu
-    padded32[HALO : HALO + frame_count, :] = glu.astype(F32)
-
-    end = HALO + frame_count
+    end = HALO + share
+    for m in range(narrow):
+        value_half = jnp.dot(normed, pin[m, :, :channels], preferred_element_type=F32)
+        gate_half = jnp.dot(normed, pin[m, :, channels:], preferred_element_type=F32)
+        glu = (value_half * jax.nn.sigmoid(gate_half)).astype(BF16)
+        padded[HALO:end, m * channels : (m + 1) * channels] = glu
+        padded32[HALO:end, m * channels : (m + 1) * channels] = glu.astype(F32)
+
     to_left = remote(
         padded.at[HALO : 2 * HALO, :],
         padded.at[end : end + HALO, :],
         hs.at[0],
         hr.at[0],
-        ((me_w + wide - 1) % wide, me_n),
+        (before // narrow, before % narrow),
     )
     to_right = remote(
-        padded.at[frame_count:end, :],
+        padded.at[share:end, :],
         padded.at[0:HALO, :],
         hs.at[1],
         hr.at[1],
-        ((me_w + 1) % wide, me_n),
+        (after // narrow, after % narrow),
     )
-    has_left = me_w > 0
-    has_right = me_w < wide - 1
+    has_left = place_now > 0
+    has_right = place_now < total_count - 1
 
     @pl.when(has_left)
     def _():
@@ -402,25 +450,33 @@
         to_right.start()
 
     half = (taps - 1) // 2
-    step_rows = 64
+    step_rows = min(32, share)
 
     def depthwise(starts):
-        def strip(c, carry):
-            lanes = pl.ds(pl.multiple_of(c * 128, 128), 128)
-            kernel_taps = depth_ref[:, lanes].astype(F32)
-            for start in starts:
-                total = jnp.zeros((step_rows, 128), F32)
-                for j in range(taps):
-                    low = start + HALO - half + j
-                    total = total + padded32[low : low + step_rows, lanes] * kernel_taps[j : j + 1, :]
-                activated[start : start + step_rows, lanes] = (
-                    total * jax.nn.sigmoid(total)
-                ).astype(BF16)
-            return carry
-
-        lax.fori_loop(0, channels // 128, strip, 0)
-
-    depthwise(range(step_rows, frame_count - step_rows, step_rows))
+        for m in range(narrow):
+
+            def strip(c, carry, m=m):
+                lanes = pl.ds(pl.multiple_of(m * channels + c * 128, 128), 128)
+                kernel_taps = taps_all[m, :, pl.ds(pl.multiple_of(c * 128, 128), 128)]
+                for start in starts:
+                    total = jnp.zeros((step_rows, 128), F32)
+                    for j in range(taps):
+                        low = start + HALO - half + j
+                        total = (
+                            total
+                            + padded32[low : low + step_rows, lanes] * kernel_taps[j : j + 1, :]
+                        )
+                    activated[start : start + step_rows, lanes] = (
+                        total * jax.nn.sigmoid(total)
+                    ).astype(BF16)
+                return carry
+
+            lax.fori_loop(0, channels // 128, strip, 0)
+
+    edges = sorted({0, share - step_rows})
+    inside = [start for start in range(0, share, step_rows) if start not in edges]
+    if inside:
+        depthwise(inside)
 
     @pl.when(has_right)
     def _():
@@ -429,7 +485,7 @@
 
     @pl.when(jnp.logical_not(has_right))
     def _():
-        padded32[end : end + HALO, :] = jnp.zeros((HALO, channels), F32)
+        padded32[end : end + HALO, :] = jnp.zeros((HALO, width), F32)
 
     @pl.when(has_left)
     def _():
@@ -438,32 +494,13 @@
 
     @pl.when(jnp.logical_not(has_left))
     def _():
-        padded32[0:HALO, :] = jnp.zeros((HALO, channels), F32)
-
-    depthwise((0, frame_count - step_rows))
-
-    def share_copy(m):
-        return remote(
-            shares.at[share_rows(m), :], shares_in.at[me_n], os_.at[m], or_.at[me_n], (me_w, m)
-        )
-
-    def share_wait(m):
-        return remote(
-            shares.at[share_rows(m), :], shares_in.at[m], os_.at[m], or_.at[m], (me_w, m)
-        )
-
-    for m in siblings:
-        shares[share_rows(m), :] = jnp.dot(
-            activated[share_rows(m), :], pout[...], preferred_element_type=F32
-        ).astype(BF16)
-        share_copy(m).start()
-    total = residual[share_rows(me_n), :] + jnp.dot(
-        activated[share_rows(me_n), :], pout[...], preferred_element_type=F32
-    )
-    for m in siblings:
-        share_wait(m).wait_recv()
-        total = total + shares_in[m].astype(F32)
-    out_ref[...] = total.astype(BF16)
+        padded32[0:HALO, :] = jnp.zeros((HALO, width), F32)
+
+    depthwise(edges)
+
+    out_ref[...] = (
+        residual[...] + jnp.dot(activated[...], pout[...], preferred_element_type=F32)
+    ).astype(BF16)
 
     def finish(i, carry):
         p = (me_w + i) % wide
@@ -474,7 +511,8 @@
     lax.fori_loop(1, wide, finish, 0)
     for m in siblings:
         mix_copy(m).wait_send()
-        share_copy(m).wait_send()
+        for copy in weight_copies(m):
+            copy.wait_send()
 
     def finish_group(g, carry):
         q = plane_of(g)
@@ -534,8 +572,8 @@
             pltpu.VMEM((width, units), BF16),
             pltpu.VMEM((units, width), BF16),
             pltpu.VMEM((width, 2, channels), BF16),
-            pltpu.VMEM((width, 2 * channels), BF16),
-            pltpu.VMEM((channels, width), BF16),
+            pltpu.VMEM((narrow, width, 2 * channels), BF16),
+            pltpu.VMEM((narrow * channels, width), BF16),
             pltpu.VMEM((frame_count, 128), F32),
             pltpu.VMEM((slot_count, dc), BF16),
             pltpu.VMEM((slot_count, width), BF16),
@@ -547,12 +585,11 @@
             pltpu.VMEM((frame_count, dc), F32),
             pltpu.VMEM((frame_count, dc), F32),
             pltpu.VMEM((frame_count, width), BF16),
-            pltpu.VMEM((frame_count, width), F32),
-            pltpu.VMEM((frame_count + 2 * HALO, channels), BF16),
-            pltpu.VMEM((frame_count + 2 * HALO, channels), F32),
-            pltpu.VMEM((frame_count, channels), BF16),
-            pltpu.VMEM((frame_count, width), BF16),
-            pltpu.VMEM((narrow, share, width), BF16),
+            pltpu.VMEM((share, width), F32),
+            pltpu.VMEM((share + 2 * HALO, narrow * channels), BF16),
+            pltpu.VMEM((share + 2 * HALO, narrow * channels), F32),
+            pltpu.VMEM((share, narrow * channels), BF16),
+            pltpu.VMEM((narrow, -(-depth_kernel.shape[0] // 8) * 8, channels), F32),
             dma((5,)),
             dma((wide,)),
             dma((wide,)),
@@ -566,6 +603,10 @@
             dma((narrow,)),
             dma((2,)),
             dma((2,)),
+            dma((narrow,)),
+            dma((narrow,)),
+            dma((narrow,)),
+            dma((narrow,)),
             dma((narrow,)),
             dma((narrow,)),
         ],

time: 68.4 us -> 71 us (1.038)
  the two profiles are of different devices: /device:TPU:25 before, /device:TPU:24 now
where the time goes in v3:
time: 71 us; the launch traced here: 70.8 us
  Pallas kernels  69.2 us (97%)
  local copies, waits for them, and re-layouts  1.67 us (2%)
    pallas_call x1, Pallas kernels, shards(): pl.pallas_call(functools.partial(block_kernel, wide, narrow, groups, cap)...  69.2 us
    unnamed x1, local copies, waits for them, and re-layouts  1.67 us

profile of v3, /device:TPU:24, one launch (start us, length us, event | category | flops | bytes accessed | tf_op | source)
XLA Modules:
  0.0 70.8 jit_solution(17620094585844856000)
XLA Ops:
  0.0 69.2 %conformer_block.1 = bf16[128,1024]{1,0:T(8,128)(2,1)} custom-call(bf16[256,1024]{1,0:T(8,128)(2,1)} %frames_ref.1, s32[2,256]{1,0:T(2,128)} %bitcast.6, f32[2,256]{1,0:T(2,128)} %bitcast.7, f32[1,1024]{1,0:T(1,128)} %bitcast.4, f32[1,1024]{1,0:T(1,128)} %bitcast.5, bf16[31,512]{1,0:T(8,128)(2,1)} %depth_ref.1, bf16[1,1024,2048]{2,1,0:T(8,128)(2,1)} %w_gate_hbm.1, ...), custom_call_target="tpu_custom_call" | custom-call | flops 13690208256 | bytes 12582912 | tf_op jit(solution)/shard_map/conformer_block/pallas_call | solution.py:565
  69.2 1.7 %copy.13 = bf16[128,1024]{1,0:T(8,128)(2,1)} copy(bf16[128,1024]{1,0:T(8,128)(2,1)} %conformer_block.1) | data formatting | bytes 524288

commit v4 on v3

--- a/solution.py
+++ b/solution.py
@@ -292,7 +292,7 @@
     def step(g, carry):
         q = plane_of(g)
 
-        @pl.when(g == 1)
+        @pl.when(g == groups - 1)
         def _():
             for load in loads[3:]:
                 load.wait()
@@ -306,9 +306,6 @@
             lax.fori_loop(0, width // 64, sort, 0)
             taps_all[me_n] = jnp.zeros(taps_all.shape[1:], F32)
             taps_all[me_n, 0:taps, :] = depth_ref[...].astype(F32)
-            for m in siblings:
-                for copy in weight_copies(m):
-                    copy.start()
 
         def take(i, c):
             s = q * size + (inner + size - i) % size
@@ -360,6 +357,9 @@
         return carry
 
     lax.fori_loop(0, groups, step, 0)
+    for m in siblings:
+        for copy in weight_copies(m):
+            copy.start()
     returned[slots(me_w), :] = sums[slots(me_w), :]
 
     mix0[...] = jnp.zeros_like(mix0)

time: 71 us -> 69.9 us (0.985)
  the two profiles are of different devices: /device:TPU:24 before, /device:TPU:0 now
where the time goes in v4:
time: 69.9 us; the launch traced here: 69.2 us
  Pallas kernels  67.5 us (97%)
  local copies, waits for them, and re-layouts  1.67 us (2%)
    pallas_call x1, Pallas kernels, shards(): pl.pallas_call(functools.partial(block_kernel, wide, narrow, groups, cap)...  67.5 us
    unnamed x1, local copies, waits for them, and re-layouts  1.67 us

profile of v4, /device:TPU:0, one launch (start us, length us, event | category | flops | bytes accessed | tf_op | source)
XLA Modules:
  0.0 69.2 jit_solution(10549266017874640460)
XLA Ops:
  0.0 67.5 %conformer_block.1 = bf16[128,1024]{1,0:T(8,128)(2,1)} custom-call(bf16[256,1024]{1,0:T(8,128)(2,1)} %frames_ref.1, s32[2,256]{1,0:T(2,128)} %bitcast.6, f32[2,256]{1,0:T(2,128)} %bitcast.7, f32[1,1024]{1,0:T(1,128)} %bitcast.4, f32[1,1024]{1,0:T(1,128)} %bitcast.5, bf16[31,512]{1,0:T(8,128)(2,1)} %depth_ref.1, bf16[1,1024,2048]{2,1,0:T(8,128)(2,1)} %w_gate_hbm.1, ...), custom_call_target="tpu_custom_call" | custom-call | flops 13690208256 | bytes 12582912 | tf_op jit(solution)/shard_map/conformer_block/pallas_call | solution.py:565
  67.6 1.7 %copy.13 = bf16[128,1024]{1,0:T(8,128)(2,1)} copy(bf16[128,1024]{1,0:T(8,128)(2,1)} %conformer_block.1) | data formatting | bytes 524288

commit v5 on v2

--- a/solution.py
+++ b/solution.py
@@ -36,6 +36,9 @@
     pin,
     pout,
     turned,
+    meta,
+    far_meta,
+    far_frames,
     outgoing,
     arrived,
     hidden,
@@ -53,6 +56,8 @@
     shares,
     shares_in,
     w_sem,
+    zs,
+    zr,
     fs,
     fr,
     xs,
@@ -135,6 +140,14 @@
             device_id_type=pl.DeviceIdType.MESH,
         )
 
+    partner = (plane + 2) % groups * size + inner
+    pl.semaphore_wait(barrier, wide - 1 + narrow - 1)
+    far_copy = remote(
+        frames_ref.at[:, my_cols], far_frames, zs.at[0], zr.at[0], (partner, me_n)
+    )
+    far_copy.start()
+    meta_copy = remote(meta, far_meta, zs.at[1], zr.at[1], (partner, me_n))
+
     id0 = ids_ref[0:1, :]
     id1 = ids_ref[1:2, :]
     lane = lax.broadcasted_iota(jnp.int32, (128, frame_count), 0)
@@ -161,49 +174,63 @@
             lane == 1, row1, jnp.where(lane == 2, gates_ref[0:1, :], gates_ref[1:2, :])
         ),
     )
+    meta[...] = stacked[0:8, :]
+    meta_copy.start()
     turned[...] = jnp.transpose(stacked)
     row0 = row0.astype(jnp.int32)
     row1 = row1.astype(jnp.int32)
 
+    def crossing(g):
+        return ((g + 1) // 2) % 2
+
     def plane_of(g):
-        return ((plane // 2 + g % 2) % 2) * 2 + (plane % 2 + g // 2) % 2
-
-    def send_copy(p):
+        return ((plane // 2 + crossing(g)) % 2) * 2 + (plane % 2 + g // 2) % 2
+
+    def near_plane(g):
+        return plane // 2 * 2 + (plane % 2 + g // 2) % 2
+
+    def send_copy(g, i):
+        p = plane_of(g) * size + i
+        home = me_w + crossing(g) * (partner - me_w)
         return remote(
             outgoing.at[slots(p), :],
-            arrived.at[slots(me_w), my_cols],
+            arrived.at[slots(home), my_cols],
             fs.at[p],
-            fr.at[me_w],
-            (p, me_n),
-        )
-
-    def recv_copy(s):
+            fr.at[home],
+            (near_plane(g) * size + i, me_n),
+        )
+
+    def recv_copy(g, i):
+        s = plane_of(g) * size + i
         return remote(
             outgoing.at[slots(s), :],
             arrived.at[slots(s), my_cols],
             fs.at[s],
             fr.at[s],
-            (s, me_n),
-        )
+            (near_plane(g) * size + i, me_n),
+        )
+
+    def dispatch(g, first, second, source):
+        q = plane_of(g)
+        place = lax.broadcasted_iota(jnp.int32, (rows, frame_count), 0) + near_plane(g) * rows
+        choose = jnp.where((place == first) | (place == second), 1.0, 0.0).astype(BF16)
+        outgoing[group_rows(q), :] = jnp.dot(
+            choose, source, preferred_element_type=F32
+        ).astype(BF16)
+        local = g // 2 == 0
+        if local:
+            own = slots(q * size + inner)
+            arrived[own, my_cols] = outgoing[own, :]
+
+        def send(i, carry):
+            send_copy(g, (inner + i) % size).start()
+            return carry
+
+        lax.fori_loop(1 if local else 0, size, send, 0)
 
     mine = frames_ref[:, my_cols]
-    for turn, g in enumerate((1, 0, 3, 2)):
-        q = plane_of(g)
-        place = lax.broadcasted_iota(jnp.int32, (rows, frame_count), 0) + q * rows
-        choose = jnp.where((place == row0) | (place == row1), 1.0, 0.0).astype(BF16)
-        outgoing[group_rows(q), :] = jnp.dot(
-            choose, mine, preferred_element_type=F32
-        ).astype(BF16)
-        if turn == 0:
-            pl.semaphore_wait(barrier, wide - 1 + narrow - 1)
-        if g == 0:
-            arrived[slots(me_w), my_cols] = outgoing[slots(me_w), :]
-
-        def send(i, carry, q=q):
-            send_copy(q * size + (inner + i) % size).start()
-            return carry
-
-        lax.fori_loop(1 if g == 0 else 0, size, send, 0)
+    dispatch(3, row0, row1, mine)
+    dispatch(0, row0, row1, mine)
 
     def forward_copy(g, q, m):
         part = arrived.at[group_rows(q), my_cols]
@@ -267,13 +294,20 @@
                 return c
 
             lax.fori_loop(0, width // 64, sort, 0)
+            far_copy.wait_recv()
+            meta_copy.wait_recv()
+            far0 = far_meta[0:1, :].astype(jnp.int32)
+            far1 = far_meta[1:2, :].astype(jnp.int32)
+            far = far_frames[...]
+            dispatch(2, far0, far1, far)
+            dispatch(1, far0, far1, far)
 
         def take(i, c):
-            s = q * size + (inner + size - i) % size
-
-            @pl.when(s != me_w)
+            other = (inner + size - i) % size
+
+            @pl.when(near_plane(g) * size + other != me_w)
             def _():
-                recv_copy(s).wait_recv()
+                recv_copy(g, other).wait_recv()
 
             return c
 
@@ -466,9 +500,7 @@
     out_ref[...] = total.astype(BF16)
 
     def finish(i, carry):
-        p = (me_w + i) % wide
-        send_copy(p).wait_send()
-        return_copy(p).wait_send()
+        return_copy((me_w + i) % wide).wait_send()
         return carry
 
     lax.fori_loop(1, wide, finish, 0)
@@ -476,8 +508,20 @@
         mix_copy(m).wait_send()
         share_copy(m).wait_send()
 
+    far_copy.wait_send()
+    meta_copy.wait_send()
+
     def finish_group(g, carry):
         q = plane_of(g)
+
+        def sent(i, c):
+            @pl.when(near_plane(g) * size + i != me_w)
+            def _():
+                send_copy(g, i).wait_send()
+
+            return c
+
+        lax.fori_loop(0, size, sent, 0)
         for m in siblings:
             forward_copy(g, q, m).wait_send()
             partial_copy(g, q, m).wait_send()
@@ -537,6 +581,9 @@
             pltpu.VMEM((width, 2 * channels), BF16),
             pltpu.VMEM((channels, width), BF16),
             pltpu.VMEM((frame_count, 128), F32),
+            pltpu.VMEM((8, frame_count), F32),
+            pltpu.VMEM((8, frame_count), F32),
+            pltpu.VMEM((frame_count, dc), BF16),
             pltpu.VMEM((slot_count, dc), BF16),
             pltpu.VMEM((slot_count, width), BF16),
             pltpu.VMEM((rows, units), BF16),
@@ -554,6 +601,8 @@
             pltpu.VMEM((frame_count, width), BF16),
             pltpu.VMEM((narrow, share, width), BF16),
             dma((5,)),
+            dma((2,)),
+            dma((2,)),
             dma((wide,)),
             dma((wide,)),
             dma((groups, narrow)),

time: 68.4 us -> 74.2 us (1.085)
  the two profiles are of different devices: /device:TPU:25 before, /device:TPU:0 now
where the time goes in v5:
time: 74.2 us; the launch traced here: 73.1 us
  Pallas kernels  71.4 us (96%)
  local copies, waits for them, and re-layouts  1.67 us (2%)
    pallas_call x1, Pallas kernels, shards(): pl.pallas_call(functools.partial(block_kernel, wide, narrow, groups, cap)...  71.4 us
    unnamed x1, local copies, waits for them, and re-layouts  1.67 us

profile of v5, /device:TPU:0, one launch (start us, length us, event | category | flops | bytes accessed | tf_op | source)
XLA Modules:
  0.0 73.1 jit_solution(6950939667629646530)
XLA Ops:
  0.0 71.4 %conformer_block.1 = bf16[128,1024]{1,0:T(8,128)(2,1)} custom-call(bf16[256,1024]{1,0:T(8,128)(2,1)} %frames_ref.1, s32[2,256]{1,0:T(2,128)} %bitcast.6, f32[2,256]{1,0:T(2,128)} %bitcast.7, f32[1,1024]{1,0:T(1,128)} %bitcast.4, f32[1,1024]{1,0:T(1,128)} %bitcast.5, bf16[31,512]{1,0:T(8,128)(2,1)} %depth_ref.1, bf16[1,1024,2048]{2,1,0:T(8,128)(2,1)} %w_gate_hbm.1, ...), custom_call_target="tpu_custom_call" | custom-call | flops 13690208256 | bytes 12582912 | tf_op jit(solution)/shard_map/conformer_block/pallas_call | solution.py:571
  71.5 1.7 %copy.13 = bf16[128,1024]{1,0:T(8,128)(2,1)} copy(bf16[128,1024]{1,0:T(8,128)(2,1)} %conformer_block.1) | data formatting | bytes 524288

commit v6 on v2

--- a/solution.py
+++ b/solution.py
@@ -36,6 +36,7 @@
     pin,
     pout,
     turned,
+    own,
     outgoing,
     arrived,
     hidden,
@@ -252,21 +253,8 @@
     siblings = [(me_n + i) % narrow for i in range(1, narrow)]
     tile = min(512, units)
 
-    def step(g, carry):
+    def take_in(g):
         q = plane_of(g)
-
-        @pl.when(g == 1)
-        def _():
-            for load in loads[3:]:
-                load.wait()
-
-            def sort(i, c):
-                r = pl.ds(pl.multiple_of(i * 64, 64), 64)
-                pin[r, :channels] = pin_raw[r, 0, :]
-                pin[r, channels:] = pin_raw[r, 1, :]
-                return c
-
-            lax.fori_loop(0, width // 64, sort, 0)
 
         def take(i, c):
             s = q * size + (inner + size - i) % size
@@ -281,43 +269,68 @@
         for m in siblings:
             forward_copy(g, q, m).start()
 
-        @pl.when(g == 0)
-        def _():
-            for load in loads[:3]:
-                load.wait()
-
+    def give_back(g):
+        q = plane_of(g)
+        total = own[...]
+        for m in siblings:
+            partial_wait(g, q, m).wait_recv()
+            total = total + partial_in[m, group_rows(q), :].astype(F32)
+        sums[group_rows(q), :] = total.astype(BF16)
+
+        def give(i, c):
+            s = q * size + (inner + size - i) % size
+
+            @pl.when(s != me_w)
+            def _():
+                return_copy(s).start()
+
+            return c
+
+        lax.fori_loop(0, size, give, 0)
+
+    take_in(0)
+    for load in loads[:3]:
+        load.wait()
+
+    def step(g, carry):
+        q = plane_of(g)
         for m in siblings:
             forward_in(g, q, m).wait_recv()
-
         x = arrived[group_rows(q), :]
         for f in range(0, units, tile):
             gate = jnp.dot(x, w_gate[:, f : f + tile], preferred_element_type=F32)
             up = jnp.dot(x, w_up[:, f : f + tile], preferred_element_type=F32)
             hidden[:, f : f + tile] = (gate * jax.nn.sigmoid(gate) * up).astype(BF16)
+
+        @pl.when(g > 0)
+        def _():
+            give_back(g - 1)
+
+        @pl.when(g < groups - 1)
+        def _():
+            take_in(g + 1)
+
         for m in siblings:
             partial[group_rows(q), cols(m)] = jnp.dot(
                 hidden[...], w_down[:, cols(m)], preferred_element_type=F32
             ).astype(BF16)
             partial_copy(g, q, m).start()
-        total = jnp.dot(hidden[...], w_down[:, my_cols], preferred_element_type=F32)
-        for m in siblings:
-            partial_wait(g, q, m).wait_recv()
-            total = total + partial_in[m, group_rows(q), :].astype(F32)
-        sums[group_rows(q), :] = total.astype(BF16)
-
-        def give(i, c):
-            s = q * size + (inner + size - i) % size
-
-            @pl.when(s != me_w)
-            def _():
-                return_copy(s).start()
-
-            return c
-
-        lax.fori_loop(0, size, give, 0)
+        own[...] = jnp.dot(hidden[...], w_down[:, my_cols], preferred_element_type=F32)
         return carry
 
     lax.fori_loop(0, groups, step, 0)
+    give_back(groups - 1)
+
+    for load in loads[3:]:
+        load.wait()
+
+    def sort(i, c):
+        r = pl.ds(pl.multiple_of(i * 64, 64), 64)
+        pin[r, :channels] = pin_raw[r, 0, :]
+        pin[r, channels:] = pin_raw[r, 1, :]
+        return c
+
+    lax.fori_loop(0, width // 64, sort, 0)
     returned[slots(me_w), :] = sums[slots(me_w), :]
 
     mix0[...] = jnp.zeros_like(mix0)
@@ -537,6 +550,7 @@
             pltpu.VMEM((width, 2 * channels), BF16),
             pltpu.VMEM((channels, width), BF16),
             pltpu.VMEM((frame_count, 128), F32),
+            pltpu.VMEM((rows, dc), F32),
             pltpu.VMEM((slot_count, dc), BF16),
             pltpu.VMEM((slot_count, width), BF16),
             pltpu.VMEM((rows, units), BF16),

time: 68.4 us -> 68.2 us (level)
  the two profiles are of different devices: /device:TPU:25 before, /device:TPU:0 now
where the time goes in v6:
time: 68.2 us; the launch traced here: 67.9 us
  Pallas kernels  66.3 us (97%)
  local copies, waits for them, and re-layouts  1.67 us (2%)
    pallas_call x1, Pallas kernels, shards(): pl.pallas_call(functools.partial(block_kernel, wide, narrow, groups, cap)...  66.3 us
    unnamed x1, local copies, waits for them, and re-layouts  1.67 us

profile of v6, /device:TPU:0, one launch (start us, length us, event | category | flops | bytes accessed | tf_op | source)
XLA Modules:
  0.0 67.9 jit_solution(14559628978808979744)
XLA Ops:
  0.0 66.3 %conformer_block.1 = bf16[128,1024]{1,0:T(8,128)(2,1)} custom-call(bf16[256,1024]{1,0:T(8,128)(2,1)} %frames_ref.1, s32[2,256]{1,0:T(2,128)} %bitcast.6, f32[2,256]{1,0:T(2,128)} %bitcast.7, f32[1,1024]{1,0:T(1,128)} %bitcast.4, f32[1,1024]{1,0:T(1,128)} %bitcast.5, bf16[31,512]{1,0:T(8,128)(2,1)} %depth_ref.1, bf16[1,1024,2048]{2,1,0:T(8,128)(2,1)} %w_gate_hbm.1, ...), custom_call_target="tpu_custom_call" | custom-call | flops 13690208256 | bytes 12582912 | tf_op jit(solution)/shard_map/conformer_block/pallas_call | solution.py:540
  66.3 1.7 %copy.13 = bf16[128,1024]{1,0:T(8,128)(2,1)} copy(bf16[128,1024]{1,0:T(8,128)(2,1)} %conformer_block.1) | data formatting | bytes 524288

commit v7 on v6

--- a/solution.py
+++ b/solution.py
@@ -204,7 +204,8 @@
             send_copy(q * size + (inner + i) % size).start()
             return carry
 
-        lax.fori_loop(1 if g == 0 else 0, size, send, 0)
+        if g < groups - 1:
+            lax.fori_loop(1 if g == 0 else 0, size, send, 0)
 
     def forward_copy(g, q, m):
         part = arrived.at[group_rows(q), my_cols]
@@ -268,6 +269,16 @@
         lax.fori_loop(0, size, take, 0)
         for m in siblings:
             forward_copy(g, q, m).start()
+
+        @pl.when(g == 1)
+        def _():
+            last = plane_of(groups - 1)
+
+            def send(i, c):
+                send_copy(last * size + (inner + i) % size).start()
+                return c
+
+            lax.fori_loop(0, size, send, 0)
 
     def give_back(g):
         q = plane_of(g)
@@ -288,7 +299,7 @@
 
         lax.fori_loop(0, size, give, 0)
 
-    take_in(0)
+    take_in(jnp.int32(0))
     for load in loads[:3]:
         load.wait()
 

time: 68.2 us -> 66.9 us (0.981)
  Pallas kernels: 66.3 us -> 65.1 us
    pallas_call x1, Pallas kernels: 66.3 us -> 65.1 us  [shards(): pl.pallas_call(functools.partial(block_kernel, wide, narrow, groups, cap)...]
where the time goes in v7:
time: 66.9 us; the launch traced here: 66.8 us
  Pallas kernels  65.1 us (97%)
  local copies, waits for them, and re-layouts  1.67 us (2%)
    pallas_call x1, Pallas kernels, shards(): pl.pallas_call(functools.partial(block_kernel, wide, narrow, groups, cap)...  65.1 us
    unnamed x1, local copies, waits for them, and re-layouts  1.67 us

profile of v7, /device:TPU:0, one launch (start us, length us, event | category | flops | bytes accessed | tf_op | source)
XLA Modules:
  0.0 66.8 jit_solution(10135021411257918132)
XLA Ops:
  0.0 65.1 %conformer_block.1 = bf16[128,1024]{1,0:T(8,128)(2,1)} custom-call(bf16[256,1024]{1,0:T(8,128)(2,1)} %frames_ref.1, s32[2,256]{1,0:T(2,128)} %bitcast.6, f32[2,256]{1,0:T(2,128)} %bitcast.7, f32[1,1024]{1,0:T(1,128)} %bitcast.4, f32[1,1024]{1,0:T(1,128)} %bitcast.5, bf16[31,512]{1,0:T(8,128)(2,1)} %depth_ref.1, bf16[1,1024,2048]{2,1,0:T(8,128)(2,1)} %w_gate_hbm.1, ...), custom_call_target="tpu_custom_call" | custom-call | flops 13690208256 | bytes 12582912 | tf_op jit(solution)/shard_map/conformer_block/pallas_call | solution.py:551
  65.1 1.7 %copy.13 = bf16[128,1024]{1,0:T(8,128)(2,1)} copy(bf16[128,1024]{1,0:T(8,128)(2,1)} %conformer_block.1) | data formatting | bytes 524288
